TPU v7x, 512 devices: a whole 4x4x16 slice. The times are simulated.
512 devices in a mesh: row: 32 (over y, z_hi, core), col: 16 (over z_lo, x).
Axes of the slice: x: 4, y: 4, z: 16 (z_hi: 4, z_lo: 4; z = z_hi * 4 + z_lo), core: 2. Of those that a mesh axis runs over, the one named last changes fastest.
Arguments:
- alignment: float32 [768, 64, 64], P('row', 'col'), may hold values from -6 to 6
- pair_state: float32 [768, 768, 128], P('row', 'col'), may hold values from -6 to 6
- pair_weights: float32 [8, 768, 768], P(None, 'row', 'col'), may hold values from 0 to 1, as said below
- align_gain: float32 [64], replicated, may hold values from 0.5 to 2
- value_weight: float32 [64, 256], replicated, may hold values from -0.75 to 0.75
- gate_weight: float32 [64, 256], replicated, may hold values from -0.75 to 0.75
- output_weight: float32 [256, 64], replicated, may hold values from -0.375 to 0.375
- outer_gain: float32 [64], replicated, may hold values from 0.5 to 2
- left_weight: float32 [64, 32], replicated, may hold values from -0.75 to 0.75
- right_weight: float32 [64, 32], replicated, may hold values from -0.75 to 0.75
- outer_weight: float32 [1024, 128], replicated, may hold values from -0.75 to 0.75
- outer_bias: float32 [128], replicated, may hold values from -3 to 3
Outputs:
- alignment_out: float32 [768, 64, 64], P('row', 'col')
- pair_out: float32 [768, 768, 128], P('row', 'col')
Inputs may be any that keep to these rules, and one draw needn't show every extreme that they name: `pair_weights`: every entry is positive, and for each head and row token the weights over the 768 column tokens sum to one.
All inputs are finite; a program needn't handle non-finite values.
Results may differ from a plain program's by a relative error of at most 0.00011.
Values sent between devices are 32-bit elements; how exact they have to be, the bound alone decides.
No kernel may reach another device: no remote copies, remote signals or barrier semaphores. Data moves between devices by JAX's collectives and lax.ppermute only.
A program may use at most 64 MiB of HBM per device.

v0:
```python
import jax
import jax.numpy as jnp
from jax import lax
from jax.sharding import PartitionSpec as P

PRECISE = lax.Precision.HIGHEST


def from_everyone(value, axis):
    count = lax.axis_size(axis)
    return lax.all_to_all(
        jnp.broadcast_to(value[None], (count, *value.shape)), axis, 0, 0, tiled=True
    )


def in_order(tiles, dim):
    tiles = jnp.moveaxis(tiles, 0, dim)
    lengths = tiles.shape
    return tiles.reshape(*lengths[:dim], lengths[dim] * lengths[dim + 1], *lengths[dim + 2 :])


def collect(value, axis, dim):
    tiles = from_everyone(value, axis)
    return in_order(tiles, dim)


def normalize(features, channel_gain):
    channel_mean = jnp.mean(features, axis=-1, keepdims=True)
    centered = features - channel_mean
    spread = jnp.mean(centered * centered, axis=-1, keepdims=True)
    return centered * lax.rsqrt(spread + 1e-05) * channel_gain


def on_device(
    alignment,
    pair_state,
    pair_weights,
    align_gain,
    value_weight,
    gate_weight,
    output_weight,
    outer_gain,
    left_weight,
    right_weight,
    outer_weight,
    outer_bias,
):
    head_count = pair_weights.shape[0]
    local_rows = alignment.shape[0]
    local_seqs = alignment.shape[1]
    channels = alignment.shape[2]
    normed = normalize(alignment, align_gain)
    flat_normed = normed.reshape(local_rows, local_seqs * channels)
    gathered = lax.all_gather(flat_normed, "row", axis=0, tiled=True)
    gathered = gathered.reshape(-1, local_seqs, channels)
    mixed_rows = jnp.einsum(
        "hij,jsc->ishc", collect(pair_weights, "col", 2), gathered, precision=PRECISE
    )
    per_head = value_weight.reshape(channels, head_count, -1)
    averaged = jnp.einsum("ishc,chd->ishd", mixed_rows, per_head, precision=PRECISE)
    gate_values = jax.nn.sigmoid(jnp.einsum("nsc,cd->nsd", normed, gate_weight, precision=PRECISE))
    gated_heads = gate_values * averaged.reshape(gate_values.shape)
    alignment_out = alignment + jnp.einsum(
        "nsd,dc->nsc", gated_heads, output_weight, precision=PRECISE
    )
    normed_out = normalize(alignment_out, outer_gain)
    left_side = jnp.einsum("nsc,cd->nsd", normed_out, left_weight, precision=PRECISE)
    right_side = jnp.einsum("nsc,cd->nsd", normed_out, right_weight, precision=PRECISE)
    factor_width = left_side.shape[2]
    columns = pair_state.shape[1]
    left_flat = left_side.transpose(1, 0, 2).reshape(local_seqs, local_rows * factor_width)
    right_rows = right_side.reshape(local_rows, local_seqs * factor_width)
    right_tokens = collect(right_rows, "row", 0)
    right_tokens = right_tokens.reshape(-1, local_seqs, factor_width)
    right_columns = lax.all_to_all(right_tokens, "col", split_axis=0, concat_axis=1, tiled=True)
    right_all = right_columns.transpose(1, 0, 2)
    left_all = collect(left_flat, "col", 0)
    sequences = left_all.shape[0]
    left_all = left_all.reshape(sequences, local_rows, factor_width)
    block_rows = 8
    left_blocks = left_all.reshape(
        sequences, local_rows // block_rows, block_rows, factor_width
    ).transpose(1, 2, 0, 3)

    def outer_block(left_block):
        product = jnp.einsum("isc,sjd->ijcd", left_block, right_all, precision=PRECISE) / sequences
        flattened = product.reshape(-1, factor_width * factor_width)
        projected = jnp.dot(
            flattened, outer_weight, precision=PRECISE, preferred_element_type=jnp.float32
        )
        return projected.reshape(block_rows, columns, -1)

    update = lax.map(outer_block, left_blocks).reshape(pair_state.shape)
    pair_out = pair_state + update + outer_bias
    return (alignment_out, pair_out)


def solution(mesh):
    return jax.shard_map(
        on_device,
        mesh=mesh,
        in_specs=(
            P("row", "col", None),
            P("row", "col", None),
            P(None, "row", "col"),
            P(),
            P(),
            P(),
            P(),
            P(),
            P(),
            P(),
            P(),
            P(),
        ),
        out_specs=(P("row", "col", None), P("row", "col", None)),
        check_vma=False,
    )
```

profile of v0, /device:TPU:8, one launch (start us, length us, event | category | flops | bytes accessed | tf_op | source)
XLA Modules:
  0.0 219.8 jit_solution(15116444611378009533)
XLA Ops:
  0.6 1.1 broadcast_in_dim.13
  1.7 2.4 %reshape.79 = f32[16,1,9216]{2,1,0:T(1,128)} reshape(f32[16,8,24,48]{3,2,1,0:T(8,128)S(1)} %broadcast_in_dim.13) | data formatting | bytes 1179648
  4.1 8.5 %all-to-all-start = ((f32[16,1,9216]{2,1,0:T(1,128)}), f32[16,1,9216]{2,1,0:T(1,128)S(1)}, u32[]{:S(2)}, u32[]{:S(2)}) async-start(f32[16,1,9216]{2,1,0:T(1,128)} %reshape.79), calls=%async_computation | async-start | bytes 1179648 | tf_op jit(solution)/shard_map/all_to_all | solution.py:11
  13.2 58.9 %all_gather.3 = f32[768,256]{1,0:T(8,128)S(1)} all-gather(f32[24,256]{1,0:T(8,128)S(1)} %reshape.62), channel_id=1, replica_groups=mesh['row'=32,'col'=16] {'row'}, dimensions={0}, use_global_device_ids=true | all-gather | bytes 811008 | tf_op jit(solution)/shard_map/all_gather | solution.py:54
  72.0 1.2 copy.71
  73.3 0.5 broadcast.67
  73.8 2.0 reduce
  75.9 0.7 reshape.80
  76.5 0.9 copy.72
  77.5 0.7 reshape.73
  78.2 0.4 copy-done.2
  78.6 1.1 convolution_bitcast_fusion.2
  79.7 0.5 convolution_bitcast_fusion.1
  80.9 0.3 fusion.24
  81.4 0.2 fusion.15
  81.8 0.8 broadcast_in_dim.19
  82.6 10.2 %all-to-all-start.2 = ((f32[32,24,128]{2,1,0:T(8,128)}), f32[32,24,128]{2,1,0:T(8,128)S(1)}, u32[]{:S(2)}, u32[]{:S(2)}) async-start(f32[32,24,128]{2,1,0:T(8,128)} %broadcast_in_dim.19), calls=%async_computation.2 | async-start | bytes 786432 | tf_op jit(solution)/shard_map/all_to_all | solution.py:11
  92.8 0.2 convolution_bitcast_fusion.3
  93.1 19.2 %all-to-all-done.2 = f32[32,24,128]{2,1,0:T(8,128)S(1)} async-done(((f32[32,24,128]{2,1,0:T(8,128)}), f32[32,24,128]{2,1,0:T(8,128)S(1)}, u32[]{:S(2)}, u32[]{:S(2)}) %all-to-all-start.2) | async-done | bytes 393248 | tf_op jit(solution)/shard_map/all_to_all | solution.py:11
  112.3 0.7 broadcast_in_dim.16
  113.0 13.8 %all-to-all-start.1 = ((f32[16,4,768]{2,1,0:T(4,128)}), f32[16,4,768]{2,1,0:T(4,128)S(1)}, u32[]{:S(2)}, u32[]{:S(2)}) async-start(f32[16,4,768]{2,1,0:T(4,128)} %broadcast_in_dim.16), calls=%async_computation.1 | async-start | bytes 393216 | tf_op jit(solution)/shard_map/all_to_all | solution.py:11
  126.8 0.7 reshape_reshape.3
  127.5 1.8 reshape.81
  129.3 8.0 %all-to-all-done.1 = f32[16,4,768]{2,1,0:T(4,128)S(1)} async-done(((f32[16,4,768]{2,1,0:T(4,128)}), f32[16,4,768]{2,1,0:T(4,128)S(1)}, u32[]{:S(2)}, u32[]{:S(2)}) %all-to-all-start.1) | async-done | bytes 196640 | tf_op jit(solution)/shard_map/all_to_all | solution.py:11
  137.2 3.7 %all-to-all-start.3 = ((f32[16,1,6144]{2,1,0:T(1,128)}), f32[16,1,6144]{2,1,0:T(1,128)S(1)}, u32[]{:S(2)}, u32[]{:S(2)}) async-start(f32[16,1,6144]{2,1,0:T(1,128)} %reshape.81), calls=%async_computation.3 | async-start | bytes 786432 | tf_op jit(solution)/shard_map/all_to_all | solution.py:75
  141.0 0.6 copy.81
  141.6 0.3 reshape_reshape_reshape.3
  141.9 0.3 copy.79
  142.2 11.7 %all-to-all-done.3 = f32[16,1,6144]{2,1,0:T(1,128)S(1)} async-done(((f32[16,1,6144]{2,1,0:T(1,128)}), f32[16,1,6144]{2,1,0:T(1,128)S(1)}, u32[]{:S(2)}, u32[]{:S(2)}) %all-to-all-start.3) | async-done | bytes 393248 | tf_op jit(solution)/shard_map/all_to_all | solution.py:75
  153.8 1.6 reduce.1
  155.4 0.8 reshape.82
  156.2 0.7 copy.86
  156.9 0.6 copy.80
  157.5 0.4 copy-done.1
  157.9 59.8 %while.10 = (s32[]{:T(128)}, f32[3,8,48,128]{3,2,1,0:T(8,128)}, f32[3,8,64,32]{2,3,1,0:T(8,128)S(1)}, f32[64,48,32]{0,1,2:T(8,128)S(1)}, f32[1024,128]{1,0:T(8,128)S(1)}, /*index=5*/s32[]{:T(128)}) while((s32[]{:T(128)}, f32[3,8,48,128]{3,2,1,0:T(8,128)}, f32[3,8,64,32]{2,3,1,0:T(8,128)S(1)}, f32[64,48,32]{0,1,2:T(8,128)S(1)}, ...), condition=%wide.region_5.6_spmd, body=%wide.region_4.5_spmd.sunk | while | flops 906362880 | bytes 11076169 | solution.py:93
  157.9 4.9 %multiply_bitcast_fusion.2 = f32[8,48,32,32]{1,2,3,0:T(8,128)} fusion(f32[64,48,32]{0,1,2:T(8,128)S(1)} %get-tuple-element.118, f32[3,8,64,32]{2,3,1,0:T(8,128)S(1)} %get-tuple-element.117, s32[]{:T(128)} %get-tuple-element.109), kind=kOutput, calls=%fused_computation.clone.1 | convolution fusion | flops 302383104 | bytes 2490372 | tf_op jit(solution)/shard_map/while/body/eval_jaxpr/isc,sjd->ijcd/dot_general | solution.py:86
  162.9 7.9 %copy.93 = f32[8,48,32,32]{3,2,1,0:T(8,128)} copy(f32[8,48,32,32]{1,2,3,0:T(8,128)} %multiply_bitcast_fusion.2) | data formatting | bytes 3145728 | tf_op jit(solution)/shard_map/while/body/eval_jaxpr/div | solution.py:86
  170.7 5.0 %reshape.84 = f32[8,48,1024]{2,1,0:T(8,128)S(1)} reshape(f32[8,48,32,32]{3,2,1,0:T(8,128)} %copy.93) | data formatting | bytes 3145728 | tf_op jit(solution)/shard_map/reshape.25
  175.8 2.1 fusion.39
  177.8 4.9 %multiply_bitcast_fusion.2 = f32[8,48,32,32]{1,2,3,0:T(8,128)} fusion(f32[64,48,32]{0,1,2:T(8,128)S(1)} %get-tuple-element.118, f32[3,8,64,32]{2,3,1,0:T(8,128)S(1)} %get-tuple-element.117, s32[]{:T(128)} %get-tuple-element.109), kind=kOutput, calls=%fused_computation.clone.1 | convolution fusion | flops 302383104 | bytes 2490372 | tf_op jit(solution)/shard_map/while/body/eval_jaxpr/isc,sjd->ijcd/dot_general | solution.py:86
  182.8 7.9 %copy.93 = f32[8,48,32,32]{3,2,1,0:T(8,128)} copy(f32[8,48,32,32]{1,2,3,0:T(8,128)} %multiply_bitcast_fusion.2) | data formatting | bytes 3145728 | tf_op jit(solution)/shard_map/while/body/eval_jaxpr/div | solution.py:86
  190.6 5.0 %reshape.84 = f32[8,48,1024]{2,1,0:T(8,128)S(1)} reshape(f32[8,48,32,32]{3,2,1,0:T(8,128)} %copy.93) | data formatting | bytes 3145728 | tf_op jit(solution)/shard_map/reshape.25
  195.7 2.1 fusion.39
  197.8 4.9 %multiply_bitcast_fusion.2 = f32[8,48,32,32]{1,2,3,0:T(8,128)} fusion(f32[64,48,32]{0,1,2:T(8,128)S(1)} %get-tuple-element.118, f32[3,8,64,32]{2,3,1,0:T(8,128)S(1)} %get-tuple-element.117, s32[]{:T(128)} %get-tuple-element.109), kind=kOutput, calls=%fused_computation.clone.1 | convolution fusion | flops 302383104 | bytes 2490372 | tf_op jit(solution)/shard_map/while/body/eval_jaxpr/isc,sjd->ijcd/dot_general | solution.py:86
  202.7 7.9 %copy.93 = f32[8,48,32,32]{3,2,1,0:T(8,128)} copy(f32[8,48,32,32]{1,2,3,0:T(8,128)} %multiply_bitcast_fusion.2) | data formatting | bytes 3145728 | tf_op jit(solution)/shard_map/while/body/eval_jaxpr/div | solution.py:86
  210.6 5.0 %reshape.84 = f32[8,48,1024]{2,1,0:T(8,128)S(1)} reshape(f32[8,48,32,32]{3,2,1,0:T(8,128)} %copy.93) | data formatting | bytes 3145728 | tf_op jit(solution)/shard_map/reshape.25
  215.6 2.1 fusion.39
  217.7 2.1 fusion.10
  (38 shorter events, 1.6 us)
Async XLA Ops:
  0.6 80.0 %copy-start = (f32[64,256]{1,0:T(8,128)S(1)}, f32[64,256]{1,0:T(8,128)}, u32[]{:S(2)}) copy-start(f32[64,256]{1,0:T(8,128)} %param.19) | copy-start | bytes 196612
  1.7 10.9 %copy-start.3 = (f32[24,4,64]{2,1,0:T(4,128)S(1)}, f32[24,4,64]{2,1,0:T(4,128)}, u32[]{:S(2)}) copy-start(f32[24,4,64]{2,1,0:T(4,128)} %param.14) | copy-start | bytes 73732
  1.7 11.2 %copy-start.6 = (f32[64]{0:T(128)S(1)}, f32[64]{0:T(128)}, u32[]{:S(2)}) copy-start(f32[64]{0:T(128)} %param.17) | copy-start | bytes 772
  4.1 69.2 %all-to-all-start = ((f32[16,1,9216]{2,1,0:T(1,128)}), f32[16,1,9216]{2,1,0:T(1,128)S(1)}, u32[]{:S(2)}, u32[]{:S(2)}) async-start(f32[16,1,9216]{2,1,0:T(1,128)} %reshape.79), calls=%async_computation | async-start | bytes 1179648 | tf_op jit(solution)/shard_map/all_to_all | solution.py:11
  12.6 60.6 %copy-start.4 = (f32[64,256]{1,0:T(8,128)S(1)}, f32[64,256]{1,0:T(8,128)}, u32[]{:S(2)}) copy-start(f32[64,256]{1,0:T(8,128)} %param.18) | copy-start | bytes 196612
  77.5 1.1 copy-start.2
  79.7 1.2 copy-start.5
  79.7 1.7 copy-start.8
  79.7 1.7 copy-start.10
  80.2 12.5 %copy-start.9 = (f32[64,32]{0,1:T(8,128)S(1)}, f32[64,32]{0,1:T(8,128)}, u32[]{:S(2)}) copy-start(f32[64,32]{0,1:T(8,128)} %param.22) | copy-start | bytes 24580
  82.6 29.7 %all-to-all-start.2 = ((f32[32,24,128]{2,1,0:T(8,128)}), f32[32,24,128]{2,1,0:T(8,128)S(1)}, u32[]{:S(2)}, u32[]{:S(2)}) async-start(f32[32,24,128]{2,1,0:T(8,128)} %broadcast_in_dim.19), calls=%async_computation.2 | async-start | bytes 786432 | tf_op jit(solution)/shard_map/all_to_all | solution.py:11
  113.0 24.2 %all-to-all-start.1 = ((f32[16,4,768]{2,1,0:T(4,128)}), f32[16,4,768]{2,1,0:T(4,128)S(1)}, u32[]{:S(2)}, u32[]{:S(2)}) async-start(f32[16,4,768]{2,1,0:T(4,128)} %broadcast_in_dim.16), calls=%async_computation.1 | async-start | bytes 393216 | tf_op jit(solution)/shard_map/all_to_all | solution.py:11
  137.2 16.6 %all-to-all-start.3 = ((f32[16,1,6144]{2,1,0:T(1,128)}), f32[16,1,6144]{2,1,0:T(1,128)S(1)}, u32[]{:S(2)}, u32[]{:S(2)}) async-start(f32[16,1,6144]{2,1,0:T(1,128)} %reshape.81), calls=%async_computation.3 | async-start | bytes 786432 | tf_op jit(solution)/shard_map/all_to_all | solution.py:75
  156.9 1.0 copy-start.1
  157.9 59.8 %copy-start.7 = (f32[128]{0:T(128)S(1)}, f32[128]{0:T(128)}, u32[]{:S(2)}) copy-start(f32[128]{0:T(128)} %param.25) | copy-start | bytes 1540
where the time goes:
time: 221 us; the launch traced here: 220 us
  blocking collectives  58.9 us (27%)
  local copies, waits for them, and re-layouts  54.9 us (25%)
  waiting for transfers between devices  38.8 us (18%)
  starting transfers between devices  36.2 us (16%)
  matrix products  23.7 us (11%)
  other arithmetic  6.28 us (3%)
    all_gather x1, blocking collectives, on_device(): gathered = lax.all_gather(flat_normed, 'row', axis=0, tiled=True)  58.9 us
    all_to_all x3, starting transfers between devices, from_everyone(): lax.all_to_all(jnp.broadcast_to(value[None], (count, *value.shape)), axis...  32.5 us
    all_to_all x3, waiting for transfers between devices, from_everyone(): lax.all_to_all(jnp.broadcast_to(value[None], (count, *value.shape)), axis...  27.2 us
    div x3, local copies, waits for them, and re-layouts, outer_block(): jnp.einsum('isc,sjd->ijcd', left_block, right_all, precision=PRECISE)  23.6 us
    another operation x3, local copies, waits for them, and re-layouts  15.1 us
    dot_general x3, matrix products, outer_block(): jnp.einsum('isc,sjd->ijcd', left_block, right_all, precision=PRECISE)  14.8 us
    all_to_all x1, waiting for transfers between devices, on_device(): lax.all_to_all(right_tokens, 'col', split_axis=0, concat_axis=1, tiled=True)  11.7 us
    unnamed x28, local copies, waits for them, and re-layouts  7.25 us
  transfers between devices with their start and end apart: 4, of which 3 were waited for; matrix products, arithmetic and copies ran while one was open for 3% of the time, Pallas kernels for 0%

commit v1 on v0

--- a/solution.py
+++ b/solution.py
@@ -51,7 +51,9 @@
     channels = alignment.shape[2]
     normed = normalize(alignment, align_gain)
     flat_normed = normed.reshape(local_rows, local_seqs * channels)
-    gathered = lax.all_gather(flat_normed, "row", axis=0, tiled=True)
+    gathered = jnp.concatenate(
+        lax.all_to_all(jnp.stack([flat_normed] * lax.axis_size("row")), "row", 0, 0), axis=0
+    )
     gathered = gathered.reshape(-1, local_seqs, channels)
     mixed_rows = jnp.einsum(
         "hij,jsc->ishc", collect(pair_weights, "col", 2), gathered, precision=PRECISE

time: 221 us -> 228 us (1.032)
  blocking collectives: 58.9 us -> 0 us
  waiting for transfers between devices: 38.8 us -> 76.4 us
  starting transfers between devices: 36.2 us -> 61.8 us
  local copies, waits for them, and re-layouts: 54.9 us -> 58 us
    all_gather x1 -> x0, blocking collectives: 58.9 us -> none  [on_device(): gathered = lax.all_gather(flat_normed, 'row', axis=0, tiled=True)]
    all_to_all x0 -> x1, waiting for transfers between devices: none -> 22 us  [on_device(): lax.all_to_all(jnp.stack([flat_normed] * lax.axis_size('row')), 'row', 0, 0)]
    all_to_all x0 -> x1, starting transfers between devices: none -> 15.7 us  [on_device(): lax.all_to_all(jnp.stack([flat_normed] * lax.axis_size('row')), 'row', 0, 0)]
    all_to_all x3, waiting for transfers between devices: 27.2 us -> 42.1 us  [from_everyone(): lax.all_to_all(jnp.broadcast_to(value[None], (count, *value.shape)), axis...]
    all_to_all x3, starting transfers between devices: 32.5 us -> 42.6 us  [from_everyone(): lax.all_to_all(jnp.broadcast_to(value[None], (count, *value.shape)), axis...]
    another operation x3 -> x7, local copies, waits for them, and re-layouts: 15.1 us -> 18.7 us
  transfers between devices with their start and end apart: 4 -> 5, of which waited for: 3 -> 5; matrix products, arithmetic and copies ran while one was open for 3% -> 4% of each run, Pallas kernels for 0% -> 0%
where the time goes in v1:
time: 228 us; the launch traced here: 227 us
  waiting for transfers between devices  76.4 us (34%)
  starting transfers between devices  61.8 us (27%)
  local copies, waits for them, and re-layouts  58 us (25%)
  matrix products  23.8 us (10%)
  other arithmetic  6.25 us (3%)
    all_to_all x3, starting transfers between devices, from_everyone(): lax.all_to_all(jnp.broadcast_to(value[None], (count, *value.shape)), axis...  42.6 us
    all_to_all x3, waiting for transfers between devices, from_everyone(): lax.all_to_all(jnp.broadcast_to(value[None], (count, *value.shape)), axis...  42.1 us
    div x3, local copies, waits for them, and re-layouts, outer_block(): jnp.einsum('isc,sjd->ijcd', left_block, right_all, precision=PRECISE)  23.6 us
    all_to_all x1, waiting for transfers between devices, on_device(): lax.all_to_all(jnp.stack([flat_normed] * lax.axis_size('row')), 'row', 0, 0)  22 us
    all_to_all x1, starting transfers between devices, on_device(): lax.all_to_all(jnp.stack([flat_normed] * lax.axis_size('row')), 'row', 0, 0)  15.7 us
    another operation x3, local copies, waits for them, and re-layouts  15.1 us
    dot_general x3, matrix products, outer_block(): jnp.einsum('isc,sjd->ijcd', left_block, right_all, precision=PRECISE)  14.9 us
    all_to_all x1, waiting for transfers between devices, on_device(): lax.all_to_all(right_tokens, 'col', split_axis=0, concat_axis=1, tiled=True)  12.4 us
  transfers between devices with their start and end apart: 5, of which 5 were waited for; matrix products, arithmetic and copies ran while one was open for 4% of the time, Pallas kernels for 0%

profile of v1, /device:TPU:8, one launch (start us, length us, event | category | flops | bytes accessed | tf_op | source)
XLA Modules:
  0.0 227.3 jit_solution(10370865455233850683)
XLA Ops:
  0.6 1.1 broadcast_in_dim.13
  1.7 2.4 %reshape.73 = f32[16,1,9216]{2,1,0:T(1,128)} reshape(f32[16,8,24,48]{3,2,1,0:T(8,128)S(1)} %broadcast_in_dim.13) | data formatting | bytes 1179648
  4.1 8.5 %all-to-all-start.1 = ((f32[16,1,9216]{2,1,0:T(1,128)}), f32[16,1,9216]{2,1,0:T(1,128)S(1)}, u32[]{:S(2)}, u32[]{:S(2)}) async-start(f32[16,1,9216]{2,1,0:T(1,128)} %reshape.73), calls=%async_computation.1 | async-start | bytes 1179648 | tf_op jit(solution)/shard_map/all_to_all | solution.py:11
  13.2 16.0 %all-to-all-done.1 = f32[16,1,9216]{2,1,0:T(1,128)S(1)} async-done(((f32[16,1,9216]{2,1,0:T(1,128)}), f32[16,1,9216]{2,1,0:T(1,128)S(1)}, u32[]{:S(2)}, u32[]{:S(2)}) %all-to-all-start.1) | async-done | bytes 589856 | tf_op jit(solution)/shard_map/all_to_all | solution.py:11
  29.2 0.9 stack.3
  30.1 15.7 %all-to-all-start = ((f32[32,24,256]{2,1,0:T(8,128)}), f32[32,24,256]{2,1,0:T(8,128)}, u32[]{:S(2)}, u32[]{:S(2)}) async-start(f32[32,24,256]{2,1,0:T(8,128)} %stack.3), calls=%async_computation | async-start | bytes 1572864 | tf_op jit(solution)/shard_map/all_to_all | solution.py:55
  45.9 0.5 broadcast.68
  46.5 2.0 reduce
  48.5 0.7 reshape.74
  49.1 0.9 copy.70
  50.1 1.5 reshape.67
  51.6 22.0 %all-to-all-done = f32[32,24,256]{2,1,0:T(8,128)} async-done(((f32[32,24,256]{2,1,0:T(8,128)}), f32[32,24,256]{2,1,0:T(8,128)}, u32[]{:S(2)}, u32[]{:S(2)}) %all-to-all-start) | async-done | bytes 786464 | tf_op jit(solution)/shard_map/all_to_all | solution.py:55
  73.5 1.9 reshape_reshape.6
  75.4 0.7 copy.71
  76.1 0.4 copy-done.2
  76.5 1.1 convolution_bitcast_fusion.2
  77.7 0.5 convolution_bitcast_fusion.1
  78.8 0.3 fusion.25
  79.7 0.8 broadcast_in_dim.19
  80.5 19.3 %all-to-all-start.3 = ((f32[32,24,128]{2,1,0:T(8,128)}), f32[32,24,128]{2,1,0:T(8,128)S(1)}, u32[]{:S(2)}, u32[]{:S(2)}) async-start(f32[32,24,128]{2,1,0:T(8,128)} %broadcast_in_dim.19), calls=%async_computation.3 | async-start | bytes 786432 | tf_op jit(solution)/shard_map/all_to_all | solution.py:11
  100.1 17.5 %all-to-all-done.3 = f32[32,24,128]{2,1,0:T(8,128)S(1)} async-done(((f32[32,24,128]{2,1,0:T(8,128)}), f32[32,24,128]{2,1,0:T(8,128)S(1)}, u32[]{:S(2)}, u32[]{:S(2)}) %all-to-all-start.3) | async-done | bytes 393248 | tf_op jit(solution)/shard_map/all_to_all | solution.py:11
  117.7 0.7 broadcast_in_dim.16
  118.4 14.8 %all-to-all-start.2 = ((f32[16,4,768]{2,1,0:T(4,128)}), f32[16,4,768]{2,1,0:T(4,128)S(1)}, u32[]{:S(2)}, u32[]{:S(2)}) async-start(f32[16,4,768]{2,1,0:T(4,128)} %broadcast_in_dim.16), calls=%async_computation.2 | async-start | bytes 393216 | tf_op jit(solution)/shard_map/all_to_all | solution.py:11
  133.2 0.7 reshape_reshape.7
  133.9 1.8 reshape.75
  135.7 8.5 %all-to-all-done.2 = f32[16,4,768]{2,1,0:T(4,128)S(1)} async-done(((f32[16,4,768]{2,1,0:T(4,128)}), f32[16,4,768]{2,1,0:T(4,128)S(1)}, u32[]{:S(2)}, u32[]{:S(2)}) %all-to-all-start.2) | async-done | bytes 196640 | tf_op jit(solution)/shard_map/all_to_all | solution.py:11
  144.1 3.6 %all-to-all-start.4 = ((f32[16,1,6144]{2,1,0:T(1,128)}), f32[16,1,6144]{2,1,0:T(1,128)S(1)}, u32[]{:S(2)}, u32[]{:S(2)}) async-start(f32[16,1,6144]{2,1,0:T(1,128)} %reshape.75), calls=%async_computation.4 | async-start | bytes 786432 | tf_op jit(solution)/shard_map/all_to_all | solution.py:77
  147.7 0.6 copy.80
  148.9 12.4 %all-to-all-done.4 = f32[16,1,6144]{2,1,0:T(1,128)S(1)} async-done(((f32[16,1,6144]{2,1,0:T(1,128)}), f32[16,1,6144]{2,1,0:T(1,128)S(1)}, u32[]{:S(2)}, u32[]{:S(2)}) %all-to-all-start.4) | async-done | bytes 393248 | tf_op jit(solution)/shard_map/all_to_all | solution.py:77
  161.2 1.5 reduce.1
  162.8 0.8 reshape.76
  163.6 0.7 copy.85
  164.3 0.6 copy.79
  164.9 0.4 copy-done.1
  165.3 59.8 %while.10 = (s32[]{:T(128)}, f32[3,8,48,128]{3,2,1,0:T(8,128)}, f32[3,8,64,32]{2,3,1,0:T(8,128)S(1)}, f32[64,48,32]{0,1,2:T(8,128)S(1)}, f32[1024,128]{1,0:T(8,128)S(1)}, /*index=5*/s32[]{:T(128)}) while((s32[]{:T(128)}, f32[3,8,48,128]{3,2,1,0:T(8,128)}, f32[3,8,64,32]{2,3,1,0:T(8,128)S(1)}, f32[64,48,32]{0,1,2:T(8,128)S(1)}, ...), condition=%wide.region_5.6_spmd, body=%wide.region_4.5_spmd.sunk | while | flops 906362880 | bytes 11076169 | solution.py:95
  165.3 5.0 %multiply_bitcast_fusion.2 = f32[8,48,32,32]{1,2,3,0:T(8,128)} fusion(f32[64,48,32]{0,1,2:T(8,128)S(1)} %get-tuple-element.118, f32[3,8,64,32]{2,3,1,0:T(8,128)S(1)} %get-tuple-element.117, s32[]{:T(128)} %get-tuple-element.109), kind=kOutput, calls=%fused_computation.clone.1 | convolution fusion | flops 302383104 | bytes 2490372 | tf_op jit(solution)/shard_map/while/body/eval_jaxpr/isc,sjd->ijcd/dot_general | solution.py:88
  170.3 7.9 %copy.92 = f32[8,48,32,32]{3,2,1,0:T(8,128)} copy(f32[8,48,32,32]{1,2,3,0:T(8,128)} %multiply_bitcast_fusion.2) | data formatting | bytes 3145728 | tf_op jit(solution)/shard_map/while/body/eval_jaxpr/div | solution.py:88
  178.2 5.0 %reshape.78 = f32[8,48,1024]{2,1,0:T(8,128)S(1)} reshape(f32[8,48,32,32]{3,2,1,0:T(8,128)} %copy.92) | data formatting | bytes 3145728 | tf_op jit(solution)/shard_map/reshape.24
  183.2 2.1 fusion.39
  185.3 5.0 %multiply_bitcast_fusion.2 = f32[8,48,32,32]{1,2,3,0:T(8,128)} fusion(f32[64,48,32]{0,1,2:T(8,128)S(1)} %get-tuple-element.118, f32[3,8,64,32]{2,3,1,0:T(8,128)S(1)} %get-tuple-element.117, s32[]{:T(128)} %get-tuple-element.109), kind=kOutput, calls=%fused_computation.clone.1 | convolution fusion | flops 302383104 | bytes 2490372 | tf_op jit(solution)/shard_map/while/body/eval_jaxpr/isc,sjd->ijcd/dot_general | solution.py:88
  190.2 7.9 %copy.92 = f32[8,48,32,32]{3,2,1,0:T(8,128)} copy(f32[8,48,32,32]{1,2,3,0:T(8,128)} %multiply_bitcast_fusion.2) | data formatting | bytes 3145728 | tf_op jit(solution)/shard_map/while/body/eval_jaxpr/div | solution.py:88
  198.1 5.0 %reshape.78 = f32[8,48,1024]{2,1,0:T(8,128)S(1)} reshape(f32[8,48,32,32]{3,2,1,0:T(8,128)} %copy.92) | data formatting | bytes 3145728 | tf_op jit(solution)/shard_map/reshape.24
  203.1 2.1 fusion.39
  205.2 5.0 %multiply_bitcast_fusion.2 = f32[8,48,32,32]{1,2,3,0:T(8,128)} fusion(f32[64,48,32]{0,1,2:T(8,128)S(1)} %get-tuple-element.118, f32[3,8,64,32]{2,3,1,0:T(8,128)S(1)} %get-tuple-element.117, s32[]{:T(128)} %get-tuple-element.109), kind=kOutput, calls=%fused_computation.clone.1 | convolution fusion | flops 302383104 | bytes 2490372 | tf_op jit(solution)/shard_map/while/body/eval_jaxpr/isc,sjd->ijcd/dot_general | solution.py:88
  210.2 7.9 %copy.92 = f32[8,48,32,32]{3,2,1,0:T(8,128)} copy(f32[8,48,32,32]{1,2,3,0:T(8,128)} %multiply_bitcast_fusion.2) | data formatting | bytes 3145728 | tf_op jit(solution)/shard_map/while/body/eval_jaxpr/div | solution.py:88
  218.1 5.0 %reshape.78 = f32[8,48,1024]{2,1,0:T(8,128)S(1)} reshape(f32[8,48,32,32]{3,2,1,0:T(8,128)} %copy.92) | data formatting | bytes 3145728 | tf_op jit(solution)/shard_map/reshape.24
  223.1 2.1 fusion.39
  225.2 2.1 fusion.11
  (41 shorter events, 2.7 us)
Async XLA Ops:
  0.6 77.9 %copy-start = (f32[64,256]{1,0:T(8,128)S(1)}, f32[64,256]{1,0:T(8,128)}, u32[]{:S(2)}) copy-start(f32[64,256]{1,0:T(8,128)} %param.19) | copy-start | bytes 196612
  1.7 10.9 %copy-start.3 = (f32[24,4,64]{2,1,0:T(4,128)S(1)}, f32[24,4,64]{2,1,0:T(4,128)}, u32[]{:S(2)}) copy-start(f32[24,4,64]{2,1,0:T(4,128)} %param.14) | copy-start | bytes 73732
  1.7 11.2 %copy-start.6 = (f32[64]{0:T(128)S(1)}, f32[64]{0:T(128)}, u32[]{:S(2)}) copy-start(f32[64]{0:T(128)} %param.17) | copy-start | bytes 772
  4.1 25.1 %all-to-all-start.1 = ((f32[16,1,9216]{2,1,0:T(1,128)}), f32[16,1,9216]{2,1,0:T(1,128)S(1)}, u32[]{:S(2)}, u32[]{:S(2)}) async-start(f32[16,1,9216]{2,1,0:T(1,128)} %reshape.73), calls=%async_computation.1 | async-start | bytes 1179648 | tf_op jit(solution)/shard_map/all_to_all | solution.py:11
  12.6 33.2 %copy-start.4 = (f32[64,256]{1,0:T(8,128)S(1)}, f32[64,256]{1,0:T(8,128)}, u32[]{:S(2)}) copy-start(f32[64,256]{1,0:T(8,128)} %param.18) | copy-start | bytes 196612
  30.1 43.4 %all-to-all-start = ((f32[32,24,256]{2,1,0:T(8,128)}), f32[32,24,256]{2,1,0:T(8,128)}, u32[]{:S(2)}, u32[]{:S(2)}) async-start(f32[32,24,256]{2,1,0:T(8,128)} %stack.3), calls=%async_computation | async-start | bytes 1572864 | tf_op jit(solution)/shard_map/all_to_all | solution.py:55
  75.4 1.1 copy-start.2
  77.6 1.2 copy-start.5
  77.6 1.7 copy-start.8
  77.6 1.7 copy-start.10
  78.1 21.6 %copy-start.9 = (f32[64,32]{0,1:T(8,128)S(1)}, f32[64,32]{0,1:T(8,128)}, u32[]{:S(2)}) copy-start(f32[64,32]{0,1:T(8,128)} %param.22) | copy-start | bytes 24580
  80.5 37.2 %all-to-all-start.3 = ((f32[32,24,128]{2,1,0:T(8,128)}), f32[32,24,128]{2,1,0:T(8,128)S(1)}, u32[]{:S(2)}, u32[]{:S(2)}) async-start(f32[32,24,128]{2,1,0:T(8,128)} %broadcast_in_dim.19), calls=%async_computation.3 | async-start | bytes 786432 | tf_op jit(solution)/shard_map/all_to_all | solution.py:11
  118.4 25.8 %all-to-all-start.2 = ((f32[16,4,768]{2,1,0:T(4,128)}), f32[16,4,768]{2,1,0:T(4,128)S(1)}, u32[]{:S(2)}, u32[]{:S(2)}) async-start(f32[16,4,768]{2,1,0:T(4,128)} %broadcast_in_dim.16), calls=%async_computation.2 | async-start | bytes 393216 | tf_op jit(solution)/shard_map/all_to_all | solution.py:11
  144.1 17.1 %all-to-all-start.4 = ((f32[16,1,6144]{2,1,0:T(1,128)}), f32[16,1,6144]{2,1,0:T(1,128)S(1)}, u32[]{:S(2)}, u32[]{:S(2)}) async-start(f32[16,1,6144]{2,1,0:T(1,128)} %reshape.75), calls=%async_computation.4 | async-start | bytes 786432 | tf_op jit(solution)/shard_map/all_to_all | solution.py:77
  164.3 1.0 copy-start.1
  165.3 59.8 %copy-start.7 = (f32[128]{0:T(128)S(1)}, f32[128]{0:T(128)}, u32[]{:S(2)}) copy-start(f32[128]{0:T(128)} %param.25) | copy-start | bytes 1540
